TPU v7x, 128 devices: a whole 4x4x4 slice. The times are simulated.
128 devices in a mesh: had: 8 (over z, core), blk: 16 (over x, y).
Axes of the slice: x: 4, y: 4, z: 4, core: 2. Of those that a mesh axis runs over, the one named last changes fastest.
Arguments:
- panel: bfloat16 [262144, 512], P(('had', 'blk')), may hold values from -100 to 100
- signs: int32 [262144], P(('had', 'blk')), may hold values from 0 to 1
- sample_rows: int32 [16, 2048], P('blk'), may hold values from 0 to 16383
Outputs:
- q_panel: bfloat16 [262144, 512], P(('had', 'blk'))
- r_sketch: float32 [512, 512], replicated
- r_gram: float32 [512, 512], replicated
All inputs are finite; a program needn't handle non-finite values.
Results may differ from a plain program's by a relative error of at most 0.0075.
The roundings to bfloat16 on the way count: a program that leaves them out, or rounds other values in their place, can miss the bound.
Values sent between devices are 32-bit elements; how exact they have to be, the bound alone decides.
No kernel may reach another device: no remote copies, remote signals or barrier semaphores. Data moves between devices by JAX's collectives and lax.ppermute only.
A program may use at most 448 MiB of HBM per device.

v0:
```python
import functools

import jax
import jax.numpy as jnp
from jax import lax
from jax.experimental import pallas as pl
from jax.experimental.pallas import tpu as pltpu
from jax.sharding import Mesh, PartitionSpec as P

LH = 32
NB = 64
GB = 128
AXES = ("z", "c", "x", "y")
CHIPS = ("z", "x", "y")
HIGHEST = lax.Precision.HIGHEST
VMEM = pl.BlockSpec(memory_space=pltpu.VMEM)
PARAMS = pltpu.CompilerParams(vmem_limit_bytes=48 * 1024 * 1024)


def dot(first, second, first_dim=1, second_dim=0, precision=None):
    return lax.dot_general(
        first,
        second,
        (((first_dim,), (second_dim,)), ((), ())),
        precision=precision,
        preferred_element_type=jnp.float32,
    )


def upper_blocks(columns):
    count = columns // GB
    return [(i, j) for i in range(count) for j in range(i, count)]


def parity(value):
    for shift in (4, 2, 1):
        value = jnp.bitwise_xor(value, jnp.right_shift(value, shift))
    return jnp.bitwise_and(value, 1)


def sketch_kernel(own_half, picks_ref, signs_ref, panel_ref, out_ref):
    rows = panel_ref.shape[0]
    group_mine = lax.axis_index("z") * lax.axis_size("c") + lax.axis_index("c")
    half = lax.axis_index("c") if own_half else 1 - lax.axis_index("c")
    lane = lax.broadcasted_iota(jnp.int32, (128, 128), 1)
    inner_lane = jnp.bitwise_and(lane, LH - 1)
    group_lane = lane // LH
    flips = (1 - 2 * signs_ref[...]).astype(jnp.float32)
    for chunk in range(out_ref.shape[0] // 256):
        strips = []
        for part in range(2):
            start = pl.multiple_of(half * out_ref.shape[0] + chunk * 256 + part * 128, 128)
            picks = jnp.broadcast_to(picks_ref[:, pl.ds(start, 128)], (128, 128)).T
            owners = jnp.right_shift(picks, rows.bit_length() - 1)
            bits = jnp.bitwise_and(jnp.bitwise_and(picks, LH - 1), inner_lane)
            bits = parity(jnp.bitwise_xor(bits, parity(jnp.bitwise_and(owners, group_mine))))
            values = (1 - 2 * bits).astype(jnp.float32)
            group = jnp.right_shift(jnp.bitwise_and(picks, rows - 1), 5) - group_lane
            strips.append((values, group))
        tiles = []
        for tile in range(rows // 128):
            flip = flips[:, tile * 128 : tile * 128 + 128]
            tiles.append(
                jnp.concatenate(
                    [jnp.where(group == 4 * tile, values * flip, 0.0).astype(jnp.bfloat16)
                     for values, group in strips],
                    axis=0,
                )
            )
        chosen = jnp.concatenate(tiles, axis=1)
        out_ref[chunk * 256 : chunk * 256 + 256, :] = dot(chosen, panel_ref[...])


def sketch_rows(own_half, picks, signs, panel):
    return pl.pallas_call(
        functools.partial(sketch_kernel, own_half),
        out_shape=jax.ShapeDtypeStruct((picks.shape[1] // 2, panel.shape[1]), jnp.float32),
        in_specs=[VMEM] * 3,
        out_specs=VMEM,
        compiler_params=PARAMS,
        name="sketch_own" if own_half else "sketch_sent",
    )(picks, signs, panel)


def pack_gram(matrix, kept_ref, sent_ref, precision):
    columns = matrix.shape[1]
    blocks = []
    for i in range(columns // GB):
        strip = dot(matrix[:, i * GB : i * GB + GB], matrix[:, i * GB :], 0, 0, precision)
        blocks += [strip[:, j * GB : j * GB + GB] for j in range(columns // GB - i)]
    first = lax.axis_index("c") == 0
    half = len(blocks) // 2
    for place in range(half):
        own = slice(place * GB, place * GB + GB)
        kept_ref[own, :] = jnp.where(first, blocks[place], blocks[place + half])
        sent_ref[own, :] = jnp.where(first, blocks[place + half], blocks[place])


def half_shape(columns):
    return jax.ShapeDtypeStruct((len(upper_blocks(columns)) // 2 * GB, GB), jnp.float32)


def sketch_gram_kernel(parts_ref, kept_ref, sent_ref):
    pack_gram(jnp.sum(parts_ref[...], axis=0), kept_ref, sent_ref, HIGHEST)


def sketch_gram(parts):
    columns = parts.shape[2]
    return pl.pallas_call(
        sketch_gram_kernel,
        out_shape=(half_shape(columns),) * 2,
        in_specs=[VMEM],
        out_specs=(VMEM, VMEM),
        compiler_params=PARAMS,
        name="sketch_gram",
    )(parts)


def times_inverse(rows_ref, inverse, buffer, out_ref, sems):
    rows, columns = rows_ref.shape
    half = columns // 2
    copies = []
    for place, start in enumerate(range(0, rows, 512)):
        own = pl.ds(start, 512)
        buffer[own, :half] = dot(
            rows_ref[own, :half], inverse[:half, :half], 1, 1
        ).astype(jnp.bfloat16)
        buffer[own, half:] = dot(rows_ref[own, :], inverse[half:, :], 1, 1).astype(jnp.bfloat16)
        copies.append(pltpu.make_async_copy(buffer.at[own, :], out_ref.at[own, :], sems.at[place]))
        copies[-1].start()
    return copies


def spread_row(tile, k):
    return jnp.broadcast_to(tile[k : k + 1, :], tile.shape)


def spread_lane(tile, c):
    return jnp.broadcast_to(tile[:, c : c + 1], tile.shape)


def factor_block(block):
    row = lax.broadcasted_iota(jnp.int32, (NB, NB), 0)
    column = lax.broadcasted_iota(jnp.int32, (NB, NB), 1)
    both = jnp.concatenate([block, (row == column).astype(jnp.float32)], axis=1)
    count = NB // 8
    work = [both[8 * u : 8 * u + 8, :] for u in range(count)]
    sub = lax.broadcasted_iota(jnp.int32, (8, 128), 0)
    done = []
    ahead = [spread_lane(work[0], c) for c in range(8)]
    for t in range(count):
        lanes = {u: [spread_lane(work[u], 8 * t + c) for c in range(8)] for u in range(t + 1, count)}
        lanes[t] = ahead
        if t + 1 < count:
            beside = [spread_lane(work[t], 8 * t + 8 + c) for c in range(8)]
            ahead = [spread_lane(work[t + 1], 8 * t + 8 + c) for c in range(8)]
        pivots = None
        for k in range(8):
            pivot = spread_row(lanes[t][k], k)
            inverse = 1.0 / pivot
            pivots = pivot if k == 0 else jnp.where(sub == k, pivot, pivots)
            across = {c: spread_row(lanes[t][c], k) for c in range(k + 1, 8)}
            pivot_row = spread_row(work[t], k)
            ratio = jnp.where(sub > k, lanes[t][k], 0.0) * inverse
            for c in range(k + 1, 8):
                lanes[t][c] = lanes[t][c] - ratio * across[c]
            if t + 1 < count:
                next_ratio = lanes[t + 1][k] * inverse
                for c in range(8):
                    entry = spread_row(beside[c], k)
                    beside[c] = beside[c] - ratio * entry
                    ahead[c] = ahead[c] - next_ratio * entry
            if k < 7:
                work[t] = work[t] - ratio * pivot_row
            for u in range(t + 1, count):
                ratio = lanes[u][k] * inverse
                for c in range(k + 1, 8):
                    lanes[u][c] = lanes[u][c] - ratio * across[c]
                work[u] = work[u] - ratio * pivot_row
        done.append(work[t] * lax.rsqrt(pivots))
    return jnp.concatenate(done, axis=0)


def split(value):
    first = value.astype(jnp.bfloat16)
    left = value - first.astype(jnp.float32)
    second = left.astype(jnp.bfloat16)
    third = (left - second.astype(jnp.float32)).astype(jnp.bfloat16)
    return first, second, third


def left_terms(value, axis):
    first, second, third = split(value)
    return jnp.concatenate([first, first, second, second, first, third], axis=axis)


def right_terms(value, axis):
    first, second, third = split(value)
    return jnp.concatenate([first, second, first, second, third, first], axis=axis)


def factor_into(scale, own_ref, other_ref, factor_ref, inverse_ref, work):
    order = work.shape[0]
    first = lax.axis_index("c") == 0
    blocks = upper_blocks(order)
    half = len(blocks) // 2
    for place in range(half):
        rows = slice(place * GB, place * GB + GB)
        own, other = own_ref[rows, :] * scale, other_ref[rows, :] * scale
        for which, block in (
            (place, jnp.where(first, own, other)),
            (place + half, jnp.where(first, other, own)),
        ):
            i, j = blocks[which]
            work[i * GB : i * GB + GB, j * GB : j * GB + GB] = block
            if i != j:
                work[j * GB : j * GB + GB, i * GB : i * GB + GB] = block.T
    eliminate(factor_ref, inverse_ref, work)


def times(first, second, first_dim=1, second_dim=0):
    return dot(left_terms(first, first_dim), right_terms(second, second_dim), first_dim, second_dim)


def factor_pair(block):
    row = lax.broadcasted_iota(jnp.int32, (NB, NB), 0)
    column = lax.broadcasted_iota(jnp.int32, (NB, NB), 1)
    zero = jnp.zeros((NB, NB), jnp.float32)
    first = factor_block(block[:NB, :NB])
    first_factor = jnp.where(row <= column, first[:, :NB], 0.0)
    first_inverse = first[:, NB:]
    above = times(first_inverse, block[:NB, NB:])
    below = times(block[NB:, :NB], first_inverse, 1, 1)
    second = factor_block(block[NB:, NB:] - times(below, above))
    second_factor = jnp.where(row <= column, second[:, :NB], 0.0)
    second_inverse = second[:, NB:]
    corner = -times(second_inverse, times(below, first_inverse))
    factor = jnp.concatenate(
        [jnp.concatenate([first_factor, above], axis=1), jnp.concatenate([zero, second_factor], axis=1)],
        axis=0,
    )
    inverse = jnp.concatenate(
        [jnp.concatenate([first_inverse, zero], axis=1), jnp.concatenate([corner, second_inverse], axis=1)],
        axis=0,
    )
    return factor, inverse


def eliminate(factor_ref, inverse_ref, work):
    order = work.shape[0]
    size = 2 * NB
    row = lax.broadcasted_iota(jnp.int32, (size, size), 0)
    column = lax.broadcasted_iota(jnp.int32, (size, size), 1)
    wide = lax.broadcasted_iota(jnp.int32, (size, order), 1)

    def apply(start, diagonal, inverse):
        own, rest = slice(start, start + size), slice(start + size, order)
        if start + size < order:
            left = dot(right_terms(work[rest, own], 1), inverse, 1, 1)
        work[own, own] = (row == column).astype(jnp.float32)
        strip = dot(inverse, right_terms(work[own, :], 0))
        inverse_ref[own, :] = jnp.where(wide < start + size, strip, 0.0).astype(jnp.bfloat16)
        factor_ref[own, :] = jnp.where(wide >= start + size, strip, 0.0)
        factor_ref[own, own] = diagonal
        if start + size < order:
            work[rest, own] = jnp.zeros((order - start - size, size), jnp.float32)
            work[rest, :] = work[rest, :] - dot(left_terms(left, 1), right_terms(strip, 0))

    def step(place, carry):
        own = pl.ds(pl.multiple_of(place * size, size), size)
        diagonal, inverse = factor_pair(work[own, own])
        inverse = left_terms(inverse, 1)
        for start in range(0, order, size):
            pl.when(place * size == start)(functools.partial(apply, start, diagonal, inverse))
        return carry

    lax.fori_loop(0, order // size, step, 0)


def whiten_kernel(
    scale, own_ref, other_ref, panel_ref, factor_ref, white_ref, kept_ref, sent_ref,
    work, inverse, buffer, sems,
):
    factor_into(scale, own_ref, other_ref, factor_ref, inverse, work)
    copies = times_inverse(panel_ref, inverse, buffer, white_ref, sems)
    pack_gram(buffer[...], kept_ref, sent_ref, None)
    for copy in copies:
        copy.wait()


def finish_kernel(
    scale, own_ref, other_ref, white_ref, factor_ref, out_ref, work, inverse, buffer, sems
):
    factor_into(scale, own_ref, other_ref, factor_ref, inverse, work)
    for copy in times_inverse(white_ref, inverse, buffer, out_ref, sems):
        copy.wait()


def factor_and_apply(kernel, name, extra, scale, own, other, matrix):
    rows, order = matrix.shape
    return pl.pallas_call(
        functools.partial(kernel, scale),
        out_shape=(
            jax.ShapeDtypeStruct((order, order), jnp.float32),
            jax.ShapeDtypeStruct(matrix.shape, jnp.bfloat16),
        )
        + extra,
        in_specs=[VMEM] * 3,
        out_specs=(VMEM, pl.BlockSpec(memory_space=pltpu.HBM)) + (VMEM,) * len(extra),
        scratch_shapes=[
            pltpu.VMEM((order, order), jnp.float32),
            pltpu.VMEM((order, order), jnp.bfloat16),
            pltpu.VMEM(matrix.shape, jnp.bfloat16),
            pltpu.SemaphoreType.DMA((rows // 512,)),
        ],
        compiler_params=PARAMS,
        name=name,
    )(own, other, matrix)


def sum_all(kept, sent):
    swap = [(0, 1), (1, 0)]
    kept = kept + lax.ppermute(sent, "c", swap)
    count = lax.axis_size(CHIPS)
    parts = kept.reshape(count, kept.shape[0] // count // 2, 2, GB)
    parts = lax.all_to_all(parts, CHIPS, 0, 0, tiled=True)
    total = jnp.sum(parts, axis=0, keepdims=True)
    parts = jnp.broadcast_to(total, parts.shape)
    own = lax.all_to_all(parts, CHIPS, 0, 0, tiled=True).reshape(kept.shape)
    return own, lax.ppermute(own, "c", swap)


def on_device(panel, signs, sample_rows):
    n_had = lax.axis_size("z") * lax.axis_size("c")
    n_blk = lax.axis_size("x") * lax.axis_size("y")
    rows_dev, columns = panel.shape
    sketch_count = sample_rows.shape[1]
    signs = signs.reshape(1, rows_dev)
    sent = sketch_rows(False, sample_rows, signs, panel)
    other = lax.ppermute(sent, "c", [(0, 1), (1, 0)])
    mine = sketch_rows(True, sample_rows, signs, panel) + other
    chips = lax.axis_size(CHIPS)
    mine = mine.reshape(chips, sketch_count // 2 // chips, columns)
    parts = lax.all_to_all(mine, CHIPS, 0, 0, tiled=True)
    own, other = sum_all(*sketch_gram(parts))
    r_sketch, whitened, kept, sent = factor_and_apply(
        whiten_kernel, "whiten", (half_shape(columns),) * 2,
        1.0 / (n_had * LH * sketch_count * n_blk), own, other, panel,
    )
    own, other = sum_all(kept, sent)
    r_gram, q_panel = factor_and_apply(
        finish_kernel, "finish", (), 1.0 / (rows_dev * n_had * n_blk), own, other, whitened
    )
    return (q_panel, r_sketch, r_gram)


def solution(mesh):
    devices = mesh.devices.reshape(4, 2, 4, 4)
    split = Mesh(devices, AXES)
    placed = (P(AXES, None), P(AXES), P(("x", "y"), None))
    return jax.shard_map(
        on_device,
        mesh=split,
        in_specs=placed,
        out_specs=(P(AXES, None), P(), P()),
        check_vma=False,
    )
```

profile of v0, /device:TPU:1, one launch (start us, length us, event | category | flops | bytes accessed | tf_op | source)
XLA Modules:
  0.0 169.0 jit_solution(3490169522086533616)
XLA Ops:
  0.6 0.0 copy-start
  0.6 1.6 copy-done
  2.2 0.7 copy-done.4
  2.9 0.7 copy-done.5
  3.6 2.5 %sketch_sent.1 = f32[1024,512]{1,0:T(8,128)S(1)} custom-call(s32[1,2048]{1,0:T(1,128)S(1)} %copy-done.4, s32[1,2048]{1,0:T(1,128)S(1)} %bitcast.10, bf16[2048,512]{1,0:T(8,128)(2,1)S(1)} %copy-done), custom_call_target="tpu_custom_call" | custom-call | tf_op jit(solution)/shard_map/sketch_sent/pallas_call | solution.py:75
  6.1 1.5 collective-permute-start
  7.6 2.5 %sketch_own.1 = f32[1024,512]{1,0:T(8,128)S(1)} custom-call(s32[1,2048]{1,0:T(1,128)S(1)} %copy-done.4, s32[1,2048]{1,0:T(1,128)S(1)} %bitcast.11, bf16[2048,512]{1,0:T(8,128)(2,1)S(1)} %copy-done), custom_call_target="tpu_custom_call" | custom-call | tf_op jit(solution)/shard_map/sketch_own/pallas_call | solution.py:75
  10.0 1.3 collective-permute-done
  11.4 0.5 add.9
  11.8 39.1 %all_to_all.25.parts_ref = f32[64,16,512]{2,1,0:T(8,128)S(1)} all-to-all(f32[64,16,512]{2,1,0:T(8,128)S(1)} %bitcast.12), channel_id=1, replica_groups=mesh['z'=4,'c'=2,'x'=4,'y'=4] {'z','x','y'}, dimensions={0} | all-to-all | bytes 4194304 | tf_op jit(solution)/shard_map/all_to_all | solution.py:344
  50.9 0.8 sketch_gram.1
  51.7 2.6 %collective-permute-start.1 = (f32[640,128]{1,0:T(8,128)S(1)}, f32[640,128]{1,0:T(8,128)S(1)}, u32[]{:S(2)}, u32[]{:S(2)}) collective-permute-start(f32[640,128]{1,0:T(8,128)S(1)} %get-tuple-element.12), channel_id=1, source_target_pairs={{0,16},{16,0},{1,17},{17,1},{2,18},{18,2},{3,19},{19,3},{4,20},{20... | collective-permute-start | bytes 983048 | tf_op jit(solution)/shard_map/ppermute | solution.py:323
  54.3 1.3 collective-permute-done.1
  55.6 16.3 %all_to_all.26 = f32[64,5,2,128]{3,2,1,0:T(2,128)S(1)} all-to-all(f32[64,5,2,128]{3,2,1,0:T(2,128)S(1)} %bitcast.13), channel_id=1, replica_groups=mesh['z'=4,'c'=2,'x'=4,'y'=4] {'z','x','y'}, dimensions={0} | all-to-all | bytes 655360 | tf_op jit(solution)/shard_map/all_to_all | solution.py:326
  71.9 0.1 reduce_sum.18
  72.1 0.1 broadcast_in_dim.4
  72.2 14.1 %all_to_all.27 = f32[64,5,2,128]{3,2,1,0:T(2,128)S(1)} all-to-all(f32[64,5,2,128]{3,2,1,0:T(2,128)S(1)} %broadcast_in_dim.4), channel_id=1, replica_groups=mesh['z'=4,'c'=2,'x'=4,'y'=4] {'z','x','y'}, dimensions={0} | all-to-all | bytes 655360 | tf_op jit(solution)/shard_map/all_to_all | solution.py:329
  86.3 3.2 %collective-permute-start.2 = (f32[640,128]{1,0:T(8,128)S(1)}, f32[640,128]{1,0:T(8,128)S(1)}, u32[]{:S(2)}, u32[]{:S(2)}) collective-permute-start(f32[640,128]{1,0:T(8,128)S(1)} %bitcast.6), channel_id=1, source_target_pairs={{0,16},{16,0},{1,17},{17,1},{2,18},{18,2},{3,19},{19,3},{4,20},{20... | collective-permute-start | bytes 983048 | tf_op jit(solution)/shard_map/ppermute | solution.py:330
  89.5 1.3 collective-permute-done.2.other_ref
  90.7 0.0 copy-done.1
  90.7 21.5 %whiten.1 = (f32[512,512]{1,0:T(8,128)}, bf16[2048,512]{1,0:T(8,128)(2,1)S(1)}, f32[640,128]{1,0:T(8,128)S(1)}, f32[640,128]{1,0:T(8,128)S(1)}) custom-call(f32[640,128]{1,0:T(8,128)S(1)} %bitcast.7, f32[640,128]{1,0:T(8,128)S(1)} %collective-permute-done.2.other_ref, bf16[2048,512]{1,0:T(8,128)(2,1)S(1)} %copy-done.1), custom_call_target="tpu_custom_call" | custom-call | tf_op jit(solution)/shard_map/whiten/pallas_call | solution.py:301
  112.2 0.0 copy-start.2
  112.2 1.3 copy-done.2
  113.5 0.4 collective-permute-start.3
  113.9 1.3 collective-permute-done.3
  115.2 14.9 %all_to_all.28 = f32[64,5,2,128]{3,2,1,0:T(2,128)S(1)} all-to-all(f32[64,5,2,128]{3,2,1,0:T(2,128)S(1)} %bitcast.14), channel_id=1, replica_groups=mesh['z'=4,'c'=2,'x'=4,'y'=4] {'z','x','y'}, dimensions={0} | all-to-all | bytes 655360 | tf_op jit(solution)/shard_map/all_to_all | solution.py:326
  130.0 0.1 reduce_sum.19
  130.2 0.1 broadcast_in_dim.5
  130.3 14.1 %all_to_all.29 = f32[64,5,2,128]{3,2,1,0:T(2,128)S(1)} all-to-all(f32[64,5,2,128]{3,2,1,0:T(2,128)S(1)} %broadcast_in_dim.5), channel_id=1, replica_groups=mesh['z'=4,'c'=2,'x'=4,'y'=4] {'z','x','y'}, dimensions={0} | all-to-all | bytes 655360 | tf_op jit(solution)/shard_map/all_to_all | solution.py:329
  144.4 3.2 %collective-permute-start.4 = (f32[640,128]{1,0:T(8,128)S(1)}, f32[640,128]{1,0:T(8,128)S(1)}, u32[]{:S(2)}, u32[]{:S(2)}) collective-permute-start(f32[640,128]{1,0:T(8,128)S(1)} %bitcast.8), channel_id=1, source_target_pairs={{0,16},{16,0},{1,17},{17,1},{2,18},{18,2},{3,19},{19,3},{4,20},{20... | collective-permute-start | bytes 983048 | tf_op jit(solution)/shard_map/ppermute | solution.py:330
  147.6 1.3 collective-permute-done.4.other_ref
  148.8 20.0 %finish.1 = (f32[512,512]{1,0:T(8,128)}, bf16[2048,512]{1,0:T(8,128)(2,1)}) custom-call(f32[640,128]{1,0:T(8,128)S(1)} %bitcast.9, f32[640,128]{1,0:T(8,128)S(1)} %collective-permute-done.4.other_ref, bf16[2048,512]{1,0:T(8,128)(2,1)S(1)} %copy-done.3), custom_call_target="tpu_custom_call" | custom-call | tf_op jit(solution)/shard_map/finish/pallas_call | solution.py:301
  (7 shorter events, 0.1 us)
Async XLA Ops:
  0.6 1.6 copy-start
  2.2 0.7 copy-start.4
  2.9 0.7 copy-start.5
  6.1 5.3 %collective-permute-start = (f32[1024,512]{1,0:T(8,128)S(1)}, f32[1024,512]{1,0:T(8,128)S(1)}, u32[]{:S(2)}, u32[]{:S(2)}) collective-permute-start(f32[1024,512]{1,0:T(8,128)S(1)} %sketch_sent.1), channel_id=1, source_target_pairs={{0,16},{16,0},{1,17},{17,1},{2,18},{18,2},{3,19},{19,3},{4,20},{20... | collective-permute-start | bytes 6291464 | tf_op jit(solution)/shard_map/ppermute | solution.py:340
  50.9 39.8 %copy-start.1 = (bf16[2048,512]{1,0:T(8,128)(2,1)S(1)}, bf16[2048,512]{1,0:T(8,128)(2,1)}, u32[]{:S(2)}) copy-start(bf16[2048,512]{1,0:T(8,128)(2,1)} %panel_ref.5) | copy-start | bytes 6291460
  51.7 3.9 %collective-permute-start.1 = (f32[640,128]{1,0:T(8,128)S(1)}, f32[640,128]{1,0:T(8,128)S(1)}, u32[]{:S(2)}, u32[]{:S(2)}) collective-permute-start(f32[640,128]{1,0:T(8,128)S(1)} %get-tuple-element.12), channel_id=1, source_target_pairs={{0,16},{16,0},{1,17},{17,1},{2,18},{18,2},{3,19},{19,3},{4,20},{20... | collective-permute-start | bytes 983048 | tf_op jit(solution)/shard_map/ppermute | solution.py:323
  86.3 4.4 %collective-permute-start.2 = (f32[640,128]{1,0:T(8,128)S(1)}, f32[640,128]{1,0:T(8,128)S(1)}, u32[]{:S(2)}, u32[]{:S(2)}) collective-permute-start(f32[640,128]{1,0:T(8,128)S(1)} %bitcast.6), channel_id=1, source_target_pairs={{0,16},{16,0},{1,17},{17,1},{2,18},{18,2},{3,19},{19,3},{4,20},{20... | collective-permute-start | bytes 983048 | tf_op jit(solution)/shard_map/ppermute | solution.py:330
  112.2 1.3 copy-start.2
  113.5 35.3 %copy-start.3 = (bf16[2048,512]{1,0:T(8,128)(2,1)S(1)}, bf16[2048,512]{1,0:T(8,128)(2,1)}, u32[]{:S(2)}) copy-start(bf16[2048,512]{1,0:T(8,128)(2,1)} %copy-done.2) | copy-start | bytes 6291460
  113.5 1.6 collective-permute-start.3
  144.4 4.4 %collective-permute-start.4 = (f32[640,128]{1,0:T(8,128)S(1)}, f32[640,128]{1,0:T(8,128)S(1)}, u32[]{:S(2)}, u32[]{:S(2)}) collective-permute-start(f32[640,128]{1,0:T(8,128)S(1)} %bitcast.8), channel_id=1, source_target_pairs={{0,16},{16,0},{1,17},{17,1},{2,18},{18,2},{3,19},{19,3},{4,20},{20... | collective-permute-start | bytes 983048 | tf_op jit(solution)/shard_map/ppermute | solution.py:330
where the time goes:
time: 169 us
  blocking collectives  98.5 us (58%)
  Pallas kernels  47.1 us (28%)
  starting transfers between devices  10.8 us (6%)
  waiting for transfers between devices  6.35 us (4%)
  local copies, waits for them, and re-layouts  4.48 us (3%)
    pallas_call x2, Pallas kernels, factor_and_apply(): pl.pallas_call(functools.partial(kernel, scale), out_shape=(jax.ShapeDtyp...  41.4 us
    all_to_all x1, blocking collectives, on_device(): parts = lax.all_to_all(mine, CHIPS, 0, 0, tiled=True)  39.1 us
    all_to_all x2, blocking collectives, sum_all(): parts = lax.all_to_all(parts, CHIPS, 0, 0, tiled=True)  31.2 us
    all_to_all x2, blocking collectives, sum_all(): own = lax.all_to_all(parts, CHIPS, 0, 0, tiled=True).reshape(kept.shape)  28.3 us
    ppermute x2, starting transfers between devices, sum_all(): return (own, lax.ppermute(own, 'c', swap))  6.32 us
    pallas_call x2, Pallas kernels, sketch_rows(): pl.pallas_call(functools.partial(sketch_kernel, own_half), out_shape=jax....  4.9 us
    unnamed x12, local copies, waits for them, and re-layouts  4.3 us
  transfers between devices with their start and end apart: 5, of which 5 were waited for; matrix products, arithmetic and copies ran while one was open for 0% of the time, Pallas kernels for 1%

commit v1 on v0

--- a/solution.py
+++ b/solution.py
@@ -38,47 +38,97 @@
     return jnp.bitwise_and(value, 1)
 
 
-def sketch_kernel(own_half, picks_ref, signs_ref, panel_ref, out_ref):
-    rows = panel_ref.shape[0]
+def choice(own_half, count, picks_ref, signs_ref, chunk):
+    rows = signs_ref.shape[1]
     group_mine = lax.axis_index("z") * lax.axis_size("c") + lax.axis_index("c")
     half = lax.axis_index("c") if own_half else 1 - lax.axis_index("c")
     lane = lax.broadcasted_iota(jnp.int32, (128, 128), 1)
     inner_lane = jnp.bitwise_and(lane, LH - 1)
     group_lane = lane // LH
     flips = (1 - 2 * signs_ref[...]).astype(jnp.float32)
-    for chunk in range(out_ref.shape[0] // 256):
-        strips = []
-        for part in range(2):
-            start = pl.multiple_of(half * out_ref.shape[0] + chunk * 256 + part * 128, 128)
-            picks = jnp.broadcast_to(picks_ref[:, pl.ds(start, 128)], (128, 128)).T
-            owners = jnp.right_shift(picks, rows.bit_length() - 1)
-            bits = jnp.bitwise_and(jnp.bitwise_and(picks, LH - 1), inner_lane)
-            bits = parity(jnp.bitwise_xor(bits, parity(jnp.bitwise_and(owners, group_mine))))
-            values = (1 - 2 * bits).astype(jnp.float32)
-            group = jnp.right_shift(jnp.bitwise_and(picks, rows - 1), 5) - group_lane
-            strips.append((values, group))
-        tiles = []
-        for tile in range(rows // 128):
-            flip = flips[:, tile * 128 : tile * 128 + 128]
-            tiles.append(
-                jnp.concatenate(
-                    [jnp.where(group == 4 * tile, values * flip, 0.0).astype(jnp.bfloat16)
-                     for values, group in strips],
-                    axis=0,
-                )
+    strips = []
+    for part in range(2):
+        start = pl.multiple_of(half * count + chunk * 256 + part * 128, 128)
+        picks = jnp.broadcast_to(picks_ref[:, pl.ds(start, 128)], (128, 128)).T
+        owners = jnp.right_shift(picks, rows.bit_length() - 1)
+        bits = jnp.bitwise_and(jnp.bitwise_and(picks, LH - 1), inner_lane)
+        bits = parity(jnp.bitwise_xor(bits, parity(jnp.bitwise_and(owners, group_mine))))
+        values = (1 - 2 * bits).astype(jnp.float32)
+        group = jnp.right_shift(jnp.bitwise_and(picks, rows - 1), 5) - group_lane
+        strips.append((values, group))
+    tiles = []
+    for tile in range(rows // 128):
+        flip = flips[:, tile * 128 : tile * 128 + 128]
+        tiles.append(
+            jnp.concatenate(
+                [jnp.where(group == 4 * tile, values * flip, 0.0).astype(jnp.bfloat16)
+                 for values, group in strips],
+                axis=0,
             )
-        chosen = jnp.concatenate(tiles, axis=1)
-        out_ref[chunk * 256 : chunk * 256 + 256, :] = dot(chosen, panel_ref[...])
-
-
-def sketch_rows(own_half, picks, signs, panel):
+        )
+    return jnp.concatenate(tiles, axis=1)
+
+
+def sketch_sent_kernel(
+    picks_hbm, signs_hbm, panel_hbm, out_ref, picks_ref, signs_ref, panel_ref, chosen, sems
+):
+    copies = [
+        pltpu.make_async_copy(source, target, sems.at[place])
+        for place, (source, target) in enumerate(
+            ((picks_hbm, picks_ref), (signs_hbm, signs_ref), (panel_hbm, panel_ref))
+        )
+    ]
+    for copy in copies:
+        copy.start()
+    copies[0].wait()
+    copies[1].wait()
+    count = out_ref.shape[0]
+    for chunk in range(count // 256):
+        chosen[chunk * 256 : chunk * 256 + 256, :] = choice(
+            False, count, picks_ref, signs_ref, chunk
+        )
+    copies[2].wait()
+    for start in range(0, count, 256):
+        out_ref[start : start + 256, :] = dot(chosen[start : start + 256, :], panel_ref[...])
+
+
+def sketch_own_kernel(picks_ref, signs_ref, panel_ref, out_ref):
+    count = out_ref.shape[0]
+    for chunk in range(count // 256):
+        out_ref[chunk * 256 : chunk * 256 + 256, :] = dot(
+            choice(True, count, picks_ref, signs_ref, chunk), panel_ref[...]
+        )
+
+
+def sketch_sent(picks, signs, panel):
+    count, (rows, columns) = picks.shape[1] // 2, panel.shape
     return pl.pallas_call(
-        functools.partial(sketch_kernel, own_half),
+        sketch_sent_kernel,
+        out_shape=(
+            jax.ShapeDtypeStruct((count, columns), jnp.float32),
+            jax.ShapeDtypeStruct(picks.shape, picks.dtype),
+            jax.ShapeDtypeStruct(signs.shape, signs.dtype),
+            jax.ShapeDtypeStruct(panel.shape, panel.dtype),
+        ),
+        in_specs=[pl.BlockSpec(memory_space=pltpu.HBM)] * 3,
+        out_specs=(VMEM,) * 4,
+        scratch_shapes=[
+            pltpu.VMEM((count, rows), jnp.bfloat16),
+            pltpu.SemaphoreType.DMA((3,)),
+        ],
+        compiler_params=PARAMS,
+        name="sketch_sent",
+    )(picks, signs, panel)
+
+
+def sketch_own(picks, signs, panel):
+    return pl.pallas_call(
+        sketch_own_kernel,
         out_shape=jax.ShapeDtypeStruct((picks.shape[1] // 2, panel.shape[1]), jnp.float32),
         in_specs=[VMEM] * 3,
         out_specs=VMEM,
         compiler_params=PARAMS,
-        name="sketch_own" if own_half else "sketch_sent",
+        name="sketch_own",
     )(picks, signs, panel)
 
 
@@ -289,33 +339,62 @@
 
 
 def finish_kernel(
-    scale, own_ref, other_ref, white_ref, factor_ref, out_ref, work, inverse, buffer, sems
+    scale, own_ref, other_ref, white_hbm, factor_ref, out_ref, work, inverse, buffer, sems, white_ref, arrived
 ):
+    arrival = pltpu.make_async_copy(white_hbm.at[pl.ds(0, white_ref.shape[0]), :], white_ref, arrived)
+    arrival.start()
     factor_into(scale, own_ref, other_ref, factor_ref, inverse, work)
+    arrival.wait()
     for copy in times_inverse(white_ref, inverse, buffer, out_ref, sems):
         copy.wait()
 
 
-def factor_and_apply(kernel, name, extra, scale, own, other, matrix):
-    rows, order = matrix.shape
+HBM = pl.BlockSpec(memory_space=pltpu.HBM)
+STRETCH = 16
+
+
+def scratch(rows, order):
+    return [
+        pltpu.VMEM((order, order), jnp.float32),
+        pltpu.VMEM((order, order), jnp.bfloat16),
+        pltpu.VMEM((rows, order), jnp.bfloat16),
+        pltpu.SemaphoreType.DMA((rows // 512,)),
+    ]
+
+
+def whiten(scale, own, other, panel):
+    rows, order = panel.shape
     return pl.pallas_call(
-        functools.partial(kernel, scale),
+        functools.partial(whiten_kernel, scale),
         out_shape=(
             jax.ShapeDtypeStruct((order, order), jnp.float32),
-            jax.ShapeDtypeStruct(matrix.shape, jnp.bfloat16),
-        )
-        + extra,
+            jax.ShapeDtypeStruct((STRETCH * rows, order), jnp.bfloat16),
+            half_shape(order),
+            half_shape(order),
+        ),
         in_specs=[VMEM] * 3,
-        out_specs=(VMEM, pl.BlockSpec(memory_space=pltpu.HBM)) + (VMEM,) * len(extra),
-        scratch_shapes=[
-            pltpu.VMEM((order, order), jnp.float32),
-            pltpu.VMEM((order, order), jnp.bfloat16),
-            pltpu.VMEM(matrix.shape, jnp.bfloat16),
-            pltpu.SemaphoreType.DMA((rows // 512,)),
-        ],
+        out_specs=(VMEM, HBM, VMEM, VMEM),
+        scratch_shapes=scratch(rows, order),
         compiler_params=PARAMS,
-        name=name,
-    )(own, other, matrix)
+        name="whiten",
+    )(own, other, panel)
+
+
+def finish(scale, own, other, whitened):
+    rows, order = whitened.shape[0] // STRETCH, whitened.shape[1]
+    return pl.pallas_call(
+        functools.partial(finish_kernel, scale),
+        out_shape=(
+            jax.ShapeDtypeStruct((order, order), jnp.float32),
+            jax.ShapeDtypeStruct((rows, order), jnp.bfloat16),
+        ),
+        in_specs=[VMEM, VMEM, HBM],
+        out_specs=(VMEM, HBM),
+        scratch_shapes=scratch(rows, order)
+        + [pltpu.VMEM((rows, order), jnp.bfloat16), pltpu.SemaphoreType.DMA],
+        compiler_params=PARAMS,
+        name="finish",
+    )(own, other, whitened)
 
 
 def sum_all(kept, sent):
@@ -336,21 +415,18 @@
     rows_dev, columns = panel.shape
     sketch_count = sample_rows.shape[1]
     signs = signs.reshape(1, rows_dev)
-    sent = sketch_rows(False, sample_rows, signs, panel)
+    sent, picks_near, signs_near, panel_near = sketch_sent(sample_rows, signs, panel)
     other = lax.ppermute(sent, "c", [(0, 1), (1, 0)])
-    mine = sketch_rows(True, sample_rows, signs, panel) + other
+    mine = sketch_own(picks_near, signs_near, panel_near) + other
     chips = lax.axis_size(CHIPS)
     mine = mine.reshape(chips, sketch_count // 2 // chips, columns)
     parts = lax.all_to_all(mine, CHIPS, 0, 0, tiled=True)
     own, other = sum_all(*sketch_gram(parts))
-    r_sketch, whitened, kept, sent = factor_and_apply(
-        whiten_kernel, "whiten", (half_shape(columns),) * 2,
-        1.0 / (n_had * LH * sketch_count * n_blk), own, other, panel,
+    r_sketch, whitened, kept, sent = whiten(
+        1.0 / (n_had * LH * sketch_count * n_blk), own, other, panel
     )
     own, other = sum_all(kept, sent)
-    r_gram, q_panel = factor_and_apply(
-        finish_kernel, "finish", (), 1.0 / (rows_dev * n_had * n_blk), own, other, whitened
-    )
+    r_gram, q_panel = finish(1.0 / (rows_dev * n_had * n_blk), own, other, whitened)
     return (q_panel, r_sketch, r_gram)
 
 

time: 169 us -> 167 us (0.988)
  local copies, waits for them, and re-layouts: 4.48 us -> 1.57 us
    unnamed x12 -> x6, local copies, waits for them, and re-layouts: 4.3 us -> 1.39 us
where the time goes in v1:
time: 167 us; the launch traced here: 166 us
  blocking collectives  98.5 us (59%)
  Pallas kernels  47.2 us (28%)
  starting transfers between devices  10.9 us (7%)
  waiting for transfers between devices  6.36 us (4%)
    all_to_all x1, blocking collectives, on_device(): parts = lax.all_to_all(mine, CHIPS, 0, 0, tiled=True)  39.1 us
    all_to_all x2, blocking collectives, sum_all(): parts = lax.all_to_all(parts, CHIPS, 0, 0, tiled=True)  31.2 us
    all_to_all x2, blocking collectives, sum_all(): own = lax.all_to_all(parts, CHIPS, 0, 0, tiled=True).reshape(kept.shape)  28.3 us
    pallas_call x1, Pallas kernels, whiten(): pl.pallas_call(functools.partial(whiten_kernel, scale), out_shape=(jax.Sh...  20 us
    pallas_call x1, Pallas kernels, finish(): pl.pallas_call(functools.partial(finish_kernel, scale), out_shape=(jax.Sh...  20 us
    ppermute x2, starting transfers between devices, sum_all(): return (own, lax.ppermute(own, 'c', swap))  6.32 us
    pallas_call x1, Pallas kernels, sketch_sent(): pl.pallas_call(sketch_sent_kernel, out_shape=(jax.ShapeDtypeStruct((count...  3.95 us
  transfers between devices with their start and end apart: 5, of which 5 were waited for; matrix products, arithmetic and copies ran while one was open for 0% of the time, Pallas kernels for 1%

profile of v1, /device:TPU:1, one launch (start us, length us, event | category | flops | bytes accessed | tf_op | source)
XLA Modules:
  0.0 166.2 jit_solution(7999811286306681526)
XLA Ops:
  0.6 0.0 copy-start.1
  0.6 0.7 copy-done.1
  1.3 0.0 copy-start.2
  1.3 0.7 copy-done.2
  2.0 4.0 %sketch_sent.1 = (f32[1024,512]{1,0:T(8,128)S(1)}, s32[1,2048]{1,0:T(1,128)S(1)}, s32[1,2048]{1,0:T(1,128)S(1)}, bf16[2048,512]{1,0:T(8,128)(2,1)S(1)}) custom-call(s32[1,2048]{1,0:T(1,128)S(1)} %copy-done.1, s32[1,2048]{1,0:T(1,128)S(1)} %bitcast.10, bf16[2048,512]{1,0:T(8,128)(2,1)} %panel_ref.1), custom_call_target="tpu_custom_call" | custom-call | tf_op jit(solution)/shard_map/sketch_sent/pallas_call | solution.py:105
  6.0 1.5 collective-permute-start
  7.5 2.5 %sketch_own.1 = f32[1024,512]{1,0:T(8,128)S(1)} custom-call(s32[1,2048]{1,0:T(1,128)S(1)} %get-tuple-element.15.picks_ref, s32[1,2048]{1,0:T(1,128)S(1)} %get-tuple-element.16.signs_ref, bf16[2048,512]{1,0:T(8,128)(2,1)S(1)} %get-tuple-element.17.panel_ref), custom_call_target="tpu_custom_call" | custom-call | tf_op jit(solution)/shard_map/sketch_own/pallas_call | solution.py:125
  9.9 1.3 collective-permute-done
  11.3 0.5 add.9
  11.8 39.1 %all_to_all.25.parts_ref = f32[64,16,512]{2,1,0:T(8,128)S(1)} all-to-all(f32[64,16,512]{2,1,0:T(8,128)S(1)} %bitcast.11), channel_id=1, replica_groups=mesh['z'=4,'c'=2,'x'=4,'y'=4] {'z','x','y'}, dimensions={0} | all-to-all | bytes 4194304 | tf_op jit(solution)/shard_map/all_to_all | solution.py:423
  50.8 0.0 copy-start
  50.8 0.8 sketch_gram.1
  51.6 2.6 %collective-permute-start.1 = (f32[640,128]{1,0:T(8,128)S(1)}, f32[640,128]{1,0:T(8,128)S(1)}, u32[]{:S(2)}, u32[]{:S(2)}) collective-permute-start(f32[640,128]{1,0:T(8,128)S(1)} %get-tuple-element.20), channel_id=1, source_target_pairs={{0,16},{16,0},{1,17},{17,1},{2,18},{18,2},{3,19},{19,3},{4,20},{20... | collective-permute-start | bytes 983048 | tf_op jit(solution)/shard_map/ppermute | solution.py:402
  54.2 1.3 collective-permute-done.1
  55.5 16.3 %all_to_all.26 = f32[64,5,2,128]{3,2,1,0:T(2,128)S(1)} all-to-all(f32[64,5,2,128]{3,2,1,0:T(2,128)S(1)} %bitcast.12), channel_id=1, replica_groups=mesh['z'=4,'c'=2,'x'=4,'y'=4] {'z','x','y'}, dimensions={0} | all-to-all | bytes 655360 | tf_op jit(solution)/shard_map/all_to_all | solution.py:405
  71.8 0.1 reduce_sum.18
  72.0 0.1 broadcast_in_dim.4
  72.1 14.1 %all_to_all.27 = f32[64,5,2,128]{3,2,1,0:T(2,128)S(1)} all-to-all(f32[64,5,2,128]{3,2,1,0:T(2,128)S(1)} %broadcast_in_dim.4), channel_id=1, replica_groups=mesh['z'=4,'c'=2,'x'=4,'y'=4] {'z','x','y'}, dimensions={0} | all-to-all | bytes 655360 | tf_op jit(solution)/shard_map/all_to_all | solution.py:408
  86.2 3.2 %collective-permute-start.2 = (f32[640,128]{1,0:T(8,128)S(1)}, f32[640,128]{1,0:T(8,128)S(1)}, u32[]{:S(2)}, u32[]{:S(2)}) collective-permute-start(f32[640,128]{1,0:T(8,128)S(1)} %bitcast.8), channel_id=1, source_target_pairs={{0,16},{16,0},{1,17},{17,1},{2,18},{18,2},{3,19},{19,3},{4,20},{20... | collective-permute-start | bytes 983048 | tf_op jit(solution)/shard_map/ppermute | solution.py:409
  89.4 1.3 collective-permute-done.2.other_ref
  90.6 0.0 copy-done
  90.6 20.0 %whiten.1 = (f32[512,512]{1,0:T(8,128)}, bf16[32768,512]{1,0:T(8,128)(2,1)}, f32[640,128]{1,0:T(8,128)S(1)}, f32[640,128]{1,0:T(8,128)S(1)}) custom-call(f32[640,128]{1,0:T(8,128)S(1)} %bitcast.9, f32[640,128]{1,0:T(8,128)S(1)} %collective-permute-done.2.other_ref, bf16[2048,512]{1,0:T(8,128)(2,1)S(1)} %copy-done), custom_call_target="tpu_custom_call" | custom-call | tf_op jit(solution)/shard_map/whiten/pallas_call | solution.py:367
  110.6 0.4 collective-permute-start.3
  111.1 1.3 collective-permute-done.3
  112.4 14.9 %all_to_all.28 = f32[64,5,2,128]{3,2,1,0:T(2,128)S(1)} all-to-all(f32[64,5,2,128]{3,2,1,0:T(2,128)S(1)} %bitcast.13), channel_id=1, replica_groups=mesh['z'=4,'c'=2,'x'=4,'y'=4] {'z','x','y'}, dimensions={0} | all-to-all | bytes 655360 | tf_op jit(solution)/shard_map/all_to_all | solution.py:405
  127.2 0.1 reduce_sum.19
  127.4 0.1 broadcast_in_dim.5
  127.5 14.1 %all_to_all.29 = f32[64,5,2,128]{3,2,1,0:T(2,128)S(1)} all-to-all(f32[64,5,2,128]{3,2,1,0:T(2,128)S(1)} %broadcast_in_dim.5), channel_id=1, replica_groups=mesh['z'=4,'c'=2,'x'=4,'y'=4] {'z','x','y'}, dimensions={0} | all-to-all | bytes 655360 | tf_op jit(solution)/shard_map/all_to_all | solution.py:408
  141.6 3.2 %collective-permute-start.4 = (f32[640,128]{1,0:T(8,128)S(1)}, f32[640,128]{1,0:T(8,128)S(1)}, u32[]{:S(2)}, u32[]{:S(2)}) collective-permute-start(f32[640,128]{1,0:T(8,128)S(1)} %bitcast.6), channel_id=1, source_target_pairs={{0,16},{16,0},{1,17},{17,1},{2,18},{18,2},{3,19},{19,3},{4,20},{20... | collective-permute-start | bytes 983048 | tf_op jit(solution)/shard_map/ppermute | solution.py:409
  144.8 1.3 collective-permute-done.4.other_ref
  146.0 20.0 %finish.1 = (f32[512,512]{1,0:T(8,128)}, bf16[2048,512]{1,0:T(8,128)(2,1)}) custom-call(f32[640,128]{1,0:T(8,128)S(1)} %bitcast.7, f32[640,128]{1,0:T(8,128)S(1)} %collective-permute-done.4.other_ref, bf16[32768,512]{1,0:T(8,128)(2,1)} %get-tuple-element.23.white_hbm), custom_call_target="tpu_custom_call" | custom-call | tf_op jit(solution)/shard_map/finish/pallas_call | solution.py:385
  (2 shorter events, 0.1 us)
Async XLA Ops:
  0.6 0.7 copy-start.1
  1.3 0.7 copy-start.2
  6.0 5.3 %collective-permute-start = (f32[1024,512]{1,0:T(8,128)S(1)}, f32[1024,512]{1,0:T(8,128)S(1)}, u32[]{:S(2)}, u32[]{:S(2)}) collective-permute-start(f32[1024,512]{1,0:T(8,128)S(1)} %get-tuple-element.18), channel_id=1, source_target_pairs={{0,16},{16,0},{1,17},{17,1},{2,18},{18,2},{3,19},{19,3},{4,20},{20... | collective-permute-start | bytes 6291464 | tf_op jit(solution)/shard_map/ppermute | solution.py:419
  50.8 39.8 %copy-start = (bf16[2048,512]{1,0:T(8,128)(2,1)S(1)}, bf16[2048,512]{1,0:T(8,128)(2,1)}, u32[]{:S(2)}) copy-start(bf16[2048,512]{1,0:T(8,128)(2,1)} %panel_ref.1) | copy-start | bytes 6291460
  51.6 3.9 %collective-permute-start.1 = (f32[640,128]{1,0:T(8,128)S(1)}, f32[640,128]{1,0:T(8,128)S(1)}, u32[]{:S(2)}, u32[]{:S(2)}) collective-permute-start(f32[640,128]{1,0:T(8,128)S(1)} %get-tuple-element.20), channel_id=1, source_target_pairs={{0,16},{16,0},{1,17},{17,1},{2,18},{18,2},{3,19},{19,3},{4,20},{20... | collective-permute-start | bytes 983048 | tf_op jit(solution)/shard_map/ppermute | solution.py:402
  86.2 4.4 %collective-permute-start.2 = (f32[640,128]{1,0:T(8,128)S(1)}, f32[640,128]{1,0:T(8,128)S(1)}, u32[]{:S(2)}, u32[]{:S(2)}) collective-permute-start(f32[640,128]{1,0:T(8,128)S(1)} %bitcast.8), channel_id=1, source_target_pairs={{0,16},{16,0},{1,17},{17,1},{2,18},{18,2},{3,19},{19,3},{4,20},{20... | collective-permute-start | bytes 983048 | tf_op jit(solution)/shard_map/ppermute | solution.py:409
  110.6 1.7 %collective-permute-start.3 = (f32[640,128]{1,0:T(8,128)S(1)}, f32[640,128]{1,0:T(8,128)S(1)}, u32[]{:S(2)}, u32[]{:S(2)}) collective-permute-start(f32[640,128]{1,0:T(8,128)S(1)} %get-tuple-element.22), channel_id=1, source_target_pairs={{0,16},{16,0},{1,17},{17,1},{2,18},{18,2},{3,19},{19,3},{4,20},{20... | collective-permute-start | bytes 983048 | tf_op jit(solution)/shard_map/ppermute | solution.py:402
  141.6 4.4 %collective-permute-start.4 = (f32[640,128]{1,0:T(8,128)S(1)}, f32[640,128]{1,0:T(8,128)S(1)}, u32[]{:S(2)}, u32[]{:S(2)}) collective-permute-start(f32[640,128]{1,0:T(8,128)S(1)} %bitcast.6), channel_id=1, source_target_pairs={{0,16},{16,0},{1,17},{17,1},{2,18},{18,2},{3,19},{19,3},{4,20},{20... | collective-permute-start | bytes 983048 | tf_op jit(solution)/shard_map/ppermute | solution.py:409

commit v2 on v1

--- a/solution.py
+++ b/solution.py
@@ -204,12 +204,13 @@
         if t + 1 < count:
             beside = [spread_lane(work[t], 8 * t + 8 + c) for c in range(8)]
             ahead = [spread_lane(work[t + 1], 8 * t + 8 + c) for c in range(8)]
-        pivots = None
+        pivots = pivot = spread_row(lanes[t][0], 0)
         for k in range(8):
-            pivot = spread_row(lanes[t][k], k)
             inverse = 1.0 / pivot
-            pivots = pivot if k == 0 else jnp.where(sub == k, pivot, pivots)
+            pivots = jnp.where(sub == k, pivot, pivots)
             across = {c: spread_row(lanes[t][c], k) for c in range(k + 1, 8)}
+            if k < 7:
+                pivot = spread_row(lanes[t][k + 1], k + 1) - (across[k + 1] * inverse) * across[k + 1]
             pivot_row = spread_row(work[t], k)
             ratio = jnp.where(sub > k, lanes[t][k], 0.0) * inverse
             for c in range(k + 1, 8):
@@ -249,7 +250,7 @@
     return jnp.concatenate([first, second, first, second, third, first], axis=axis)
 
 
-def factor_into(scale, own_ref, other_ref, factor_ref, inverse_ref, work):
+def factor_into(scale, own_ref, other_ref, factor_ref, inverse_ref, work, run=None):
     order = work.shape[0]
     first = lax.axis_index("c") == 0
     blocks = upper_blocks(order)
@@ -265,7 +266,7 @@
             work[i * GB : i * GB + GB, j * GB : j * GB + GB] = block
             if i != j:
                 work[j * GB : j * GB + GB, i * GB : i * GB + GB] = block.T
-    eliminate(factor_ref, inverse_ref, work)
+    (run or eliminate)(factor_ref, inverse_ref, work)
 
 
 def times(first, second, first_dim=1, second_dim=0):
@@ -327,6 +328,29 @@
     lax.fori_loop(0, order // size, step, 0)
 
 
+def eliminate_whole(factor_ref, inverse_ref, work):
+    order = work.shape[0]
+    row = lax.broadcasted_iota(jnp.int32, (NB, NB), 0)
+    column = lax.broadcasted_iota(jnp.int32, (NB, NB), 1)
+    wide = lax.broadcasted_iota(jnp.int32, (NB, order), 1)
+    for end in range(NB, order + 1, NB):
+        own = slice(end - NB, end)
+        rest = slice(end, order)
+        both = factor_block(work[own, own])
+        diagonal = jnp.where(row <= column, both[:, :NB], 0.0)
+        inverse = left_terms(both[:, NB:], 1)
+        if end < order:
+            left = dot(right_terms(work[rest, own], 1), inverse, 1, 1)
+        work[own, own] = (row == column).astype(jnp.float32)
+        strip = dot(inverse, right_terms(work[own, :], 0))
+        inverse_ref[own, :] = jnp.where(wide < end, strip, 0.0).astype(jnp.bfloat16)
+        factor_ref[own, :] = jnp.where(wide >= end, strip, 0.0)
+        factor_ref[own, own] = diagonal
+        if end < order:
+            work[rest, own] = jnp.zeros((order - end, NB), jnp.float32)
+            work[rest, :] = work[rest, :] - dot(left_terms(left, 1), right_terms(strip, 0))
+
+
 def whiten_kernel(
     scale, own_ref, other_ref, panel_ref, factor_ref, white_ref, kept_ref, sent_ref,
     work, inverse, buffer, sems,
@@ -343,7 +367,7 @@
 ):
     arrival = pltpu.make_async_copy(white_hbm.at[pl.ds(0, white_ref.shape[0]), :], white_ref, arrived)
     arrival.start()
-    factor_into(scale, own_ref, other_ref, factor_ref, inverse, work)
+    factor_into(scale, own_ref, other_ref, factor_ref, inverse, work, eliminate_whole)
     arrival.wait()
     for copy in times_inverse(white_ref, inverse, buffer, out_ref, sems):
         copy.wait()

time: 167 us -> 165 us (0.988)
  no operation moved by 1% of the time
where the time goes in v2:
time: 165 us
  blocking collectives  98.6 us (60%)
  Pallas kernels  45.7 us (28%)
  starting transfers between devices  10.8 us (7%)
  waiting for transfers between devices  6.35 us (4%)
    all_to_all x1, blocking collectives, on_device(): parts = lax.all_to_all(mine, CHIPS, 0, 0, tiled=True)  39.1 us
    all_to_all x2, blocking collectives, sum_all(): parts = lax.all_to_all(parts, CHIPS, 0, 0, tiled=True)  31.2 us
    all_to_all x2, blocking collectives, sum_all(): own = lax.all_to_all(parts, CHIPS, 0, 0, tiled=True).reshape(kept.shape)  28.3 us
    pallas_call x1, Pallas kernels, whiten(): pl.pallas_call(functools.partial(whiten_kernel, scale), out_shape=(jax.Sh...  19.9 us
    pallas_call x1, Pallas kernels, finish(): pl.pallas_call(functools.partial(finish_kernel, scale), out_shape=(jax.Sh...  18.5 us
    ppermute x2, starting transfers between devices, sum_all(): return (own, lax.ppermute(own, 'c', swap))  6.27 us
    pallas_call x1, Pallas kernels, sketch_sent(): pl.pallas_call(sketch_sent_kernel, out_shape=(jax.ShapeDtypeStruct((count...  3.95 us
  transfers between devices with their start and end apart: 5, of which 5 were waited for; matrix products, arithmetic and copies ran while one was open for 0% of the time, Pallas kernels for 1%

profile of v2, /device:TPU:1, one launch (start us, length us, event | category | flops | bytes accessed | tf_op | source)
XLA Modules:
  0.0 164.7 jit_solution(11963725005495381477)
XLA Ops:
  0.6 0.0 copy-start.1
  0.6 0.7 copy-done.1
  1.3 0.0 copy-start.2
  1.3 0.7 copy-done.2
  2.0 4.0 %sketch_sent.1 = (f32[1024,512]{1,0:T(8,128)S(1)}, s32[1,2048]{1,0:T(1,128)S(1)}, s32[1,2048]{1,0:T(1,128)S(1)}, bf16[2048,512]{1,0:T(8,128)(2,1)S(1)}) custom-call(s32[1,2048]{1,0:T(1,128)S(1)} %copy-done.1, s32[1,2048]{1,0:T(1,128)S(1)} %bitcast.10, bf16[2048,512]{1,0:T(8,128)(2,1)} %panel_ref.1), custom_call_target="tpu_custom_call" | custom-call | tf_op jit(solution)/shard_map/sketch_sent/pallas_call | solution.py:105
  6.0 1.5 collective-permute-start
  7.5 2.5 %sketch_own.1 = f32[1024,512]{1,0:T(8,128)S(1)} custom-call(s32[1,2048]{1,0:T(1,128)S(1)} %get-tuple-element.15.picks_ref, s32[1,2048]{1,0:T(1,128)S(1)} %get-tuple-element.16.signs_ref, bf16[2048,512]{1,0:T(8,128)(2,1)S(1)} %get-tuple-element.17.panel_ref), custom_call_target="tpu_custom_call" | custom-call | tf_op jit(solution)/shard_map/sketch_own/pallas_call | solution.py:125
  9.9 1.3 collective-permute-done
  11.3 0.5 add.9
  11.8 39.1 %all_to_all.25.parts_ref = f32[64,16,512]{2,1,0:T(8,128)S(1)} all-to-all(f32[64,16,512]{2,1,0:T(8,128)S(1)} %bitcast.11), channel_id=1, replica_groups=mesh['z'=4,'c'=2,'x'=4,'y'=4] {'z','x','y'}, dimensions={0} | all-to-all | bytes 4194304 | tf_op jit(solution)/shard_map/all_to_all | solution.py:447
  50.8 0.0 copy-start
  50.8 0.8 sketch_gram.1
  51.6 2.6 %collective-permute-start.1 = (f32[640,128]{1,0:T(8,128)S(1)}, f32[640,128]{1,0:T(8,128)S(1)}, u32[]{:S(2)}, u32[]{:S(2)}) collective-permute-start(f32[640,128]{1,0:T(8,128)S(1)} %get-tuple-element.20), channel_id=1, source_target_pairs={{0,16},{16,0},{1,17},{17,1},{2,18},{18,2},{3,19},{19,3},{4,20},{20... | collective-permute-start | bytes 983048 | tf_op jit(solution)/shard_map/ppermute | solution.py:426
  54.2 1.3 collective-permute-done.1
  55.5 16.3 %all_to_all.26 = f32[64,5,2,128]{3,2,1,0:T(2,128)S(1)} all-to-all(f32[64,5,2,128]{3,2,1,0:T(2,128)S(1)} %bitcast.12), channel_id=1, replica_groups=mesh['z'=4,'c'=2,'x'=4,'y'=4] {'z','x','y'}, dimensions={0} | all-to-all | bytes 655360 | tf_op jit(solution)/shard_map/all_to_all | solution.py:429
  71.8 0.1 reduce_sum.18
  72.0 0.1 broadcast_in_dim.4
  72.1 14.1 %all_to_all.27 = f32[64,5,2,128]{3,2,1,0:T(2,128)S(1)} all-to-all(f32[64,5,2,128]{3,2,1,0:T(2,128)S(1)} %broadcast_in_dim.4), channel_id=1, replica_groups=mesh['z'=4,'c'=2,'x'=4,'y'=4] {'z','x','y'}, dimensions={0} | all-to-all | bytes 655360 | tf_op jit(solution)/shard_map/all_to_all | solution.py:432
  86.2 3.2 %collective-permute-start.2 = (f32[640,128]{1,0:T(8,128)S(1)}, f32[640,128]{1,0:T(8,128)S(1)}, u32[]{:S(2)}, u32[]{:S(2)}) collective-permute-start(f32[640,128]{1,0:T(8,128)S(1)} %bitcast.8), channel_id=1, source_target_pairs={{0,16},{16,0},{1,17},{17,1},{2,18},{18,2},{3,19},{19,3},{4,20},{20... | collective-permute-start | bytes 983048 | tf_op jit(solution)/shard_map/ppermute | solution.py:433
  89.4 1.3 collective-permute-done.2.other_ref
  90.6 0.0 copy-done
  90.6 19.9 %whiten.1 = (f32[512,512]{1,0:T(8,128)}, bf16[32768,512]{1,0:T(8,128)(2,1)}, f32[640,128]{1,0:T(8,128)S(1)}, f32[640,128]{1,0:T(8,128)S(1)}) custom-call(f32[640,128]{1,0:T(8,128)S(1)} %bitcast.9, f32[640,128]{1,0:T(8,128)S(1)} %collective-permute-done.2.other_ref, bf16[2048,512]{1,0:T(8,128)(2,1)S(1)} %copy-done), custom_call_target="tpu_custom_call" | custom-call | tf_op jit(solution)/shard_map/whiten/pallas_call | solution.py:391
  110.5 0.5 collective-permute-start.3
  111.0 1.3 collective-permute-done.3
  112.3 14.9 %all_to_all.28 = f32[64,5,2,128]{3,2,1,0:T(2,128)S(1)} all-to-all(f32[64,5,2,128]{3,2,1,0:T(2,128)S(1)} %bitcast.13), channel_id=1, replica_groups=mesh['z'=4,'c'=2,'x'=4,'y'=4] {'z','x','y'}, dimensions={0} | all-to-all | bytes 655360 | tf_op jit(solution)/shard_map/all_to_all | solution.py:429
  127.2 0.1 reduce_sum.19
  127.3 0.1 broadcast_in_dim.5
  127.4 14.2 %all_to_all.29 = f32[64,5,2,128]{3,2,1,0:T(2,128)S(1)} all-to-all(f32[64,5,2,128]{3,2,1,0:T(2,128)S(1)} %broadcast_in_dim.5), channel_id=1, replica_groups=mesh['z'=4,'c'=2,'x'=4,'y'=4] {'z','x','y'}, dimensions={0} | all-to-all | bytes 655360 | tf_op jit(solution)/shard_map/all_to_all | solution.py:432
  141.6 3.1 %collective-permute-start.4 = (f32[640,128]{1,0:T(8,128)S(1)}, f32[640,128]{1,0:T(8,128)S(1)}, u32[]{:S(2)}, u32[]{:S(2)}) collective-permute-start(f32[640,128]{1,0:T(8,128)S(1)} %bitcast.6), channel_id=1, source_target_pairs={{0,16},{16,0},{1,17},{17,1},{2,18},{18,2},{3,19},{19,3},{4,20},{20... | collective-permute-start | bytes 983048 | tf_op jit(solution)/shard_map/ppermute | solution.py:433
  144.7 1.3 collective-permute-done.4.other_ref
  146.0 18.5 %finish.1 = (f32[512,512]{1,0:T(8,128)}, bf16[2048,512]{1,0:T(8,128)(2,1)}) custom-call(f32[640,128]{1,0:T(8,128)S(1)} %bitcast.7, f32[640,128]{1,0:T(8,128)S(1)} %collective-permute-done.4.other_ref, bf16[32768,512]{1,0:T(8,128)(2,1)} %get-tuple-element.23.white_hbm), custom_call_target="tpu_custom_call" | custom-call | tf_op jit(solution)/shard_map/finish/pallas_call | solution.py:409
  (2 shorter events, 0.1 us)
Async XLA Ops:
  0.6 0.7 copy-start.1
  1.3 0.7 copy-start.2
  6.0 5.3 %collective-permute-start = (f32[1024,512]{1,0:T(8,128)S(1)}, f32[1024,512]{1,0:T(8,128)S(1)}, u32[]{:S(2)}, u32[]{:S(2)}) collective-permute-start(f32[1024,512]{1,0:T(8,128)S(1)} %get-tuple-element.18), channel_id=1, source_target_pairs={{0,16},{16,0},{1,17},{17,1},{2,18},{18,2},{3,19},{19,3},{4,20},{20... | collective-permute-start | bytes 6291464 | tf_op jit(solution)/shard_map/ppermute | solution.py:443
  50.8 39.8 %copy-start = (bf16[2048,512]{1,0:T(8,128)(2,1)S(1)}, bf16[2048,512]{1,0:T(8,128)(2,1)}, u32[]{:S(2)}) copy-start(bf16[2048,512]{1,0:T(8,128)(2,1)} %panel_ref.1) | copy-start | bytes 6291460
  51.6 3.9 %collective-permute-start.1 = (f32[640,128]{1,0:T(8,128)S(1)}, f32[640,128]{1,0:T(8,128)S(1)}, u32[]{:S(2)}, u32[]{:S(2)}) collective-permute-start(f32[640,128]{1,0:T(8,128)S(1)} %get-tuple-element.20), channel_id=1, source_target_pairs={{0,16},{16,0},{1,17},{17,1},{2,18},{18,2},{3,19},{19,3},{4,20},{20... | collective-permute-start | bytes 983048 | tf_op jit(solution)/shard_map/ppermute | solution.py:426
  86.2 4.4 %collective-permute-start.2 = (f32[640,128]{1,0:T(8,128)S(1)}, f32[640,128]{1,0:T(8,128)S(1)}, u32[]{:S(2)}, u32[]{:S(2)}) collective-permute-start(f32[640,128]{1,0:T(8,128)S(1)} %bitcast.8), channel_id=1, source_target_pairs={{0,16},{16,0},{1,17},{17,1},{2,18},{18,2},{3,19},{19,3},{4,20},{20... | collective-permute-start | bytes 983048 | tf_op jit(solution)/shard_map/ppermute | solution.py:433
  110.5 1.7 %collective-permute-start.3 = (f32[640,128]{1,0:T(8,128)S(1)}, f32[640,128]{1,0:T(8,128)S(1)}, u32[]{:S(2)}, u32[]{:S(2)}) collective-permute-start(f32[640,128]{1,0:T(8,128)S(1)} %get-tuple-element.22), channel_id=1, source_target_pairs={{0,16},{16,0},{1,17},{17,1},{2,18},{18,2},{3,19},{19,3},{4,20},{20... | collective-permute-start | bytes 983048 | tf_op jit(solution)/shard_map/ppermute | solution.py:426
  141.6 4.4 %collective-permute-start.4 = (f32[640,128]{1,0:T(8,128)S(1)}, f32[640,128]{1,0:T(8,128)S(1)}, u32[]{:S(2)}, u32[]{:S(2)}) collective-permute-start(f32[640,128]{1,0:T(8,128)S(1)} %bitcast.6), channel_id=1, source_target_pairs={{0,16},{16,0},{1,17},{17,1},{2,18},{18,2},{3,19},{19,3},{4,20},{20... | collective-permute-start | bytes 983048 | tf_op jit(solution)/shard_map/ppermute | solution.py:433
